TPU v7x, 32 devices: a whole 2x2x4 slice. The times are simulated.
32 devices in a mesh: slab: 16 (over z, y, core), angle: 2 (over x).
Axes of the slice: x: 2, y: 2, z: 4, core: 2. Of those that a mesh axis runs over, the one named last changes fastest.
Arguments:
- object_density: bfloat16 [2, 128, 32, 320], P(None, 'slab', 'angle'), may hold values from -6 to 6
- resampling_matrices: bfloat16 [2, 64, 128], replicated, may hold values from -0.109375 to 0.109375
- receiving_tile_number: int32 [2, 16, 2], replicated, may hold values from 0 to 4
- illumination_modes: bfloat16 [4, 2, 256, 256], replicated, may hold values from -3 to 3
- window_corners: int32 [2, 16, 2], P('angle', 'slab'), may hold values from 1 to 63
- observed_power: float32 [2, 16, 256, 256], P('angle', 'slab'), may hold values from 0.5 to 2
Outputs:
- vol_grad: float32 [2, 128, 32, 320], P(None, 'slab', 'angle')
- probe_grad: float32 [4, 2, 256, 256], P(None, None, 'slab')
- power_mismatch: float32 [2, 16, 256, 256], P('angle', 'slab')
- locus_derivative: float32 [2, 16, 2], P('angle', 'slab')
All inputs are finite; a program needn't handle non-finite values.
Results may differ from a plain program's by a relative error of at most 0.00035.
Values sent between devices are 32-bit elements; how exact they have to be, the bound alone decides.
A program may use at most 64 MiB of HBM per device.

v0:
```python
import functools
import math

import jax
import jax.numpy as jnp
import numpy as np
from jax import lax
from jax.experimental import pallas as pl
from jax.experimental.pallas import tpu as pltpu
from jax.sharding import PartitionSpec as P

NUB = 5
INNER = 2
MID = 2
MESH = pl.DeviceIdType.MESH
VMEM = pl.BlockSpec(memory_space=pltpu.VMEM)
SMEM = pl.BlockSpec(memory_space=pltpu.SMEM)
VMEM_BYTES = 48 * 1024 * 1024


def remote(src, dst, send, recv, axis, peer):
    return pltpu.make_async_remote_copy(
        src_ref=src, dst_ref=dst, send_sem=send, recv_sem=recv,
        device_id={axis: peer}, device_id_type=MESH,
    )


def greet(n_slab, n_angle, me_s, me_a):
    barrier = pltpu.get_barrier_semaphore()
    for off in range(1, n_angle):
        pl.semaphore_signal(barrier, inc=1, device_id={"angle": lax.rem(me_a + off, n_angle)}, device_id_type=MESH)

    @pl.loop(1, n_slab)
    def _(off):
        pl.semaphore_signal(barrier, inc=1, device_id={"slab": lax.rem(me_s + off, n_slab)}, device_id_type=MESH)

    pl.semaphore_wait(barrier, n_slab + n_angle - 2)


def gather_kernel(n_slab, n_angle, blocks, hot, out, got, xbuf, xs, xr, as_, ar, zs, zr, ys, yr, cs, cr):
    n_out = n_slab // (MID * INNER)
    me_s, me_a = lax.axis_index("slab"), lax.axis_index("angle")
    me_z, me_y, me_c = me_s // (MID * INNER), lax.rem(me_s // INNER, MID), lax.rem(me_s, INNER)
    greet(n_slab, n_angle, me_s, me_a)

    def xcopy(off):
        peer = lax.rem(me_a + off, n_angle)
        return remote(blocks.at[peer], xbuf.at[off], xs.at[off], xr.at[off], "angle", peer)

    def acopy(step, off):
        peer = lax.rem(me_s + off, n_slab)
        src = blocks.at[me_a, peer] if step == 0 else xbuf.at[step, peer]
        source = lax.rem(me_a + n_angle - step, n_angle)
        return remote(src, got.at[source, me_s], as_.at[step, off], ar.at[step, off], "slab", peer)

    for off in range(1, n_angle):
        xcopy(off).start()

    @pl.loop(1, n_slab)
    def _(off):
        acopy(0, off).start()

    got[me_a, me_s] = blocks[me_a, me_s]
    for step in range(1, n_angle):
        xcopy(step).wait_recv()

        @pl.loop(1, n_slab)
        def _(off):
            acopy(step, off).start()

        got[lax.rem(me_a + n_angle - step, n_angle), me_s] = xbuf[step, me_s]
    for step in range(n_angle):

        @pl.loop(1, n_slab)
        def _(off):
            acopy(step, off).wait_recv()

    rows, z_cells = blocks.shape[2], blocks.shape[3]

    def add(i, acc):
        for j in range(n_angle):
            item = got[j, i]
            acc = tuple(acc[d] + hot[(i * n_angle + j) * NUB + d] * item for d in range(NUB))
        return acc

    acc = lax.fori_loop(0, n_slab, add, tuple(jnp.zeros((rows, z_cells), jnp.float32) for _ in range(NUB)))
    for d in range(NUB):
        out[me_z, me_y, me_c, d] = acc[d]

    def to_slab(z, y, c):
        return (z * MID + y) * INNER + c

    def zcopy(off):
        piece = out.at[me_z, me_y, me_c]
        return remote(piece, piece, zs.at[off], zr.at[off], "slab", to_slab(lax.rem(me_z + off, n_out), me_y, me_c))

    def ycopy(off):
        piece = out.at[lax.rem(me_z + n_out - off, n_out), me_y, me_c]
        return remote(piece, piece, ys.at[off], yr.at[off], "slab", to_slab(me_z, 1 - me_y, me_c))

    def ccopy(off, flip):
        row = 1 - me_y if flip else me_y
        piece = out.at[lax.rem(me_z + n_out - off, n_out), row, me_c]
        return remote(piece, piece, cs.at[flip, off], cr.at[flip, off], "slab", to_slab(me_z, me_y, 1 - me_c))

    ycopy(0).start()
    for off in range(1, n_out):
        zcopy(off).start()
    ccopy(0, 0).start()
    for off in range(1, n_out):
        zcopy(off).wait_recv()
        ycopy(off).start()
        ccopy(off, 0).start()
    for off in range(n_out):
        ycopy(off).wait_recv()
        ccopy(off, 1).start()
    for off in range(n_out):
        ccopy(off, 0).wait_recv()
        ccopy(off, 1).wait_recv()
        ycopy(off).wait_send()
        ccopy(off, 0).wait_send()
        ccopy(off, 1).wait_send()
    for off in range(1, n_out):
        zcopy(off).wait_send()
    for off in range(1, n_angle):
        xcopy(off).wait_send()
    for step in range(n_angle):

        @pl.loop(1, n_slab)
        def _(off):
            acopy(step, off).wait_send()


def reduce_kernel(
    n_slab, n_angle, pg, q, hot, vin, pr,
    p1, s1, p2, s2, p3, q1, t1, q2, t2, q3, t3, q4, disp, got,
    ps, pr_, pzs, pzr, ds, dr, vs, vr, qs, qr, qxs, qxr, qzs, qzr, qgs, qgr,
):
    n_out = n_slab // (MID * INNER)
    me_s, me_a = lax.axis_index("slab"), lax.axis_index("angle")
    me_z, me_y, me_c = me_s // (MID * INNER), lax.rem(me_s // INNER, MID), lax.rem(me_s, INNER)
    greet(n_slab, n_angle, me_s, me_a)
    planes = q.shape[0] // n_angle

    def to_slab(z, y, c):
        return (z * MID + y) * INNER + c

    core_peer = to_slab(me_z, me_y, 1 - me_c)
    mid_peer = to_slab(me_z, 1 - me_y, me_c)
    p_core = remote(pg.at[:, :, 1 - me_c], p1, ps.at[0], pr_.at[0], "slab", core_peer)
    p_core.start()
    q_core = remote(q.at[:, :, :, 1 - me_c], q1, qs.at[0], qr.at[0], "slab", core_peer)
    q_core.start()
    p_core.wait_recv()
    s1[...] = pg[:, :, me_c] + p1[...]
    p_mid = remote(s1.at[:, 1 - me_y], p2, ps.at[1], pr_.at[1], "slab", mid_peer)
    p_mid.start()
    q_core.wait_recv()
    t1[...] = q[:, :, :, me_c] + q1[...]

    def qx(off):
        peer = lax.rem(me_a + off, n_angle)
        return remote(t1.at[pl.ds(peer * planes, planes)], q2.at[off], qxs.at[off], qxr.at[off], "angle", peer)

    for off in range(1, n_angle):
        qx(off).start()
    p_mid.wait_recv()
    s2[...] = s1[:, me_y] + p2[...]

    def pz(off):
        z = lax.rem(me_z + off, n_out)
        return remote(s2.at[z], p3.at[off], pzs.at[off], pzr.at[off], "slab", to_slab(z, me_y, me_c))

    for off in range(1, n_out):
        pz(off).start()
    total = s2[me_z]
    for off in range(1, n_out):
        pz(off).wait_recv()
        total = total + p3[off]

    @pl.loop(0, n_slab)
    def _(i):
        for j in range(n_angle):
            base = (i * n_angle + j) * NUB
            block = hot[base] * total[0]
            for d in range(1, NUB):
                block = block + hot[base + d] * total[d]
            disp[i, j] = block

    def dcopy(off):
        peer = lax.rem(me_s + off, n_slab)
        return remote(disp.at[peer], got.at[:, me_s], ds.at[off], dr.at[off], "slab", peer)

    @pl.loop(1, n_slab)
    def _(off):
        dcopy(off).start()

    for j in range(n_angle):
        got[j, me_s] = disp[me_s, j]

    t2[...] = t1[pl.ds(me_a * planes, planes)]
    for off in range(1, n_angle):
        qx(off).wait_recv()
        t2[...] += q2[off]
    q_mid = remote(t2.at[:, :, 1 - me_y], q3, qs.at[1], qr.at[1], "slab", mid_peer)
    q_mid.start()

    @pl.loop(1, n_slab)
    def _(off):
        dcopy(off).wait_recv()

    def vx(off):
        peer = lax.rem(me_a + off, n_angle)
        return remote(got.at[peer], vin.at[me_a], vs.at[off], vr.at[off], "angle", peer)

    for off in range(1, n_angle):
        vx(off).start()
    vin[me_a] = got[me_a]
    q_mid.wait_recv()
    t3[...] = t2[:, :, me_y] + q3[...]

    def qz(off):
        z = lax.rem(me_z + off, n_out)
        return remote(t3.at[:, z], q4.at[off], qzs.at[off], qzr.at[off], "slab", to_slab(z, me_y, me_c))

    for off in range(1, n_out):
        qz(off).start()
    probe = t3[:, me_z]
    for off in range(1, n_out):
        qz(off).wait_recv()
        probe = probe + q4[off]
    mine = pl.ds(me_a * planes, planes)
    pr[mine] = probe

    def qg(off):
        return remote(pr.at[mine], pr.at[mine], qgs.at[off], qgr.at[off], "angle", lax.rem(me_a + off, n_angle))

    for off in range(1, n_angle):
        qg(off).start()
    for off in range(1, n_angle):
        qg(off).wait_recv()
        vx(off).wait_recv()
        qg(off).wait_send()
        vx(off).wait_send()
        qx(off).wait_send()
    for off in range(1, n_out):
        pz(off).wait_send()
        qz(off).wait_send()

    @pl.loop(1, n_slab)
    def _(off):
        dcopy(off).wait_send()

    p_core.wait_send()
    q_core.wait_send()
    p_mid.wait_send()
    q_mid.wait_send()


def split(x):
    high = x.astype(jnp.bfloat16)
    return high, (x - high.astype(jnp.float32)).astype(jnp.bfloat16)


def dot3(a, b):
    def dot(x, y):
        return jnp.dot(x, y, preferred_element_type=jnp.float32)

    return dot(a[0], b[0]) + (dot(a[0], b[1]) + dot(a[1], b[0]))


def spot_kernel(corner, gathered, probe, power, tabs, grad, pterm, resid_out, shift, det, trans, far, inten, tgrad):
    n_slab, _, rows, z_cells = gathered.shape
    side = probe.shape[2]
    modes = probe.shape[0]
    det_cols = det.shape[1]
    lanes = det.shape[2]
    per = n_slab // 2
    cols = per * rows
    col, row = corner[0], corner[1]
    for k in range(n_slab):
        for d in range(NUB):
            at = d * cols + (k % per) * rows
            det[k // per, at : at + rows, :z_cells] = gathered[k, d]
    for c in range(2):
        det[c, :, z_cells:] = jnp.zeros((det_cols, lanes - z_cells), jnp.float32)
        moved = pltpu.roll(det[c], lanes - row, 1)
        det[c] = pltpu.roll(moved, det_cols - col, 0)
    absorb = jnp.exp(-det[1, :side, :side])
    phase = det[0, :side, :side]
    trans[0] = absorb * jnp.cos(phase)
    trans[1] = absorb * jnp.sin(phase)
    inten[...] = -power[...]
    left = (tabs[0], tabs[1])
    right = (tabs[2], tabs[3])

    @pl.loop(0, modes)
    def _(m):
        pr_, pi_ = probe[m, 0].astype(jnp.float32), probe[m, 1].astype(jnp.float32)
        tr, ti = trans[0], trans[1]
        stacked = jnp.concatenate([pr_ * tr - pi_ * ti, pr_ * ti + pi_ * tr], axis=0)
        mid = dot3(left, split(stacked))
        both = jnp.concatenate([mid[:side], mid[side:]], axis=1)
        field = dot3(split(both), right)
        far[m] = field
        fr, fi = field[:, :side], field[:, side:]
        inten[...] += fr * fr + fi * fi

    resid_out[...] = inten[...]
    tgrad[...] = jnp.zeros_like(tgrad)

    @pl.loop(0, modes)
    def _(m):
        weight = 2.0 * inten[...]
        pull = jnp.concatenate([far[m, :, :side] * weight, far[m, :, side:] * weight], axis=0)
        mid = dot3(right, split(pull))
        both = jnp.concatenate([mid[:side], mid[side:]], axis=1)
        back = dot3(split(both), left)
        er, ei = back[:, :side], back[:, side:]
        tr, ti = trans[0], trans[1]
        pterm[m, 0] = er * tr + ei * ti
        pterm[m, 1] = ei * tr - er * ti
        pr_, pi_ = probe[m, 0].astype(jnp.float32), probe[m, 1].astype(jnp.float32)
        tgrad[0] += pr_ * er + pi_ * ei
        tgrad[1] += pr_ * ei - pi_ * er

    tr, ti = trans[0], trans[1]
    ga, gb = tgrad[0], tgrad[1]
    patch = (gb * tr - ga * ti, -(ga * tr + gb * ti))
    shift_col = jnp.float32(0.0)
    shift_row = jnp.float32(0.0)
    for c in range(2):
        here = det[c]
        dcol = pltpu.roll(here, det_cols - 1, 0)[:side, :side] - pltpu.roll(here, 1, 0)[:side, :side]
        drow = pltpu.roll(here, lanes - 1, 1)[:side, :side] - pltpu.roll(here, 1, 1)[:side, :side]
        shift_col += jnp.sum(patch[c] * dcol)
        shift_row += jnp.sum(patch[c] * drow)
    shift[0] = shift_col * 0.5 / side
    shift[1] = shift_row * 0.5 / side
    for c in range(2):
        det[c] = jnp.zeros((det_cols, lanes), jnp.float32)
        det[c, :side, :side] = patch[c]
        det[c] = pltpu.roll(pltpu.roll(det[c], row, 1), col, 0)
    for k in range(n_slab):
        for d in range(NUB):
            at = d * cols + (k % per) * rows
            grad[k, d] = det[k // per, at : at + rows, :z_cells]


def tables(length):
    ids = np.outer(np.arange(length), np.arange(length)) % length
    phases = ids * (2.0 * math.pi / length)
    c, s = np.cos(phases) / math.sqrt(length), np.sin(phases) / math.sqrt(length)
    left = np.block([[c, s], [-s, c]])
    parts = []
    for table in (left, left.T):
        high = table.astype(jnp.bfloat16)
        parts += [high, (table - high.astype(np.float64)).astype(jnp.bfloat16)]
    return jnp.asarray(np.stack(parts))


def local(object_density, resampling_matrices, receiving_tile_number, illumination_modes, window_corners, observed_power):
    n_angle = lax.axis_size("angle")
    n_slab = lax.axis_size("slab")
    n_out = n_slab // (MID * INNER)
    my_angle = lax.axis_index("angle")
    x_cells = object_density.shape[1]
    y_here = object_density.shape[2]
    z_cells = object_density.shape[3]
    tile_rows = resampling_matrices.shape[2]
    blk_cols = resampling_matrices.shape[1]
    modes, _, side, _ = illumination_modes.shape
    rows = 2 * blk_cols // n_slab
    per_slab = side // n_slab
    lanes = (z_cells + 127) // 128 * 128
    f32 = jnp.float32
    dma = pltpu.SemaphoreType.DMA

    tile = object_density.reshape(2, tile_rows, z_cells)
    blocks = jnp.einsum("auk,ckz->acuz", resampling_matrices, tile, preferred_element_type=f32)
    blocks = blocks.reshape(n_angle, n_slab, rows, z_cells)
    ids = lax.dynamic_index_in_dim(receiving_tile_number, my_angle, 0, keepdims=False).reshape(-1)
    hot = (ids[:, None] == jnp.arange(NUB, dtype=jnp.int32)[None, :]).astype(f32).reshape(-1)

    gathered = pl.pallas_call(
        functools.partial(gather_kernel, n_slab, n_angle),
        out_shape=jax.ShapeDtypeStruct((n_out, MID, INNER, NUB, rows, z_cells), f32),
        in_specs=[VMEM, SMEM],
        out_specs=VMEM,
        scratch_shapes=[
            pltpu.VMEM((n_angle, n_slab, rows, z_cells), f32),
            pltpu.VMEM((n_angle, n_slab, rows, z_cells), f32),
            dma((n_angle,)), dma((n_angle,)),
            dma((n_angle, n_slab)), dma((n_angle, n_slab)),
            dma((n_out,)), dma((n_out,)),
            dma((n_out,)), dma((n_out,)),
            dma((2, n_out)), dma((2, n_out)),
        ],
        compiler_params=pltpu.CompilerParams(collective_id=0, has_side_effects=True, vmem_limit_bytes=VMEM_BYTES),
    )(blocks, hot)

    grad, pterm, resid, shift = pl.pallas_call(
        spot_kernel,
        out_shape=(
            jax.ShapeDtypeStruct((n_slab, NUB, rows, z_cells), f32),
            jax.ShapeDtypeStruct((modes, 2, side, side), f32),
            jax.ShapeDtypeStruct((side, side), f32),
            jax.ShapeDtypeStruct((2,), f32),
        ),
        in_specs=[SMEM, VMEM, VMEM, VMEM, VMEM],
        out_specs=(VMEM, VMEM, VMEM, SMEM),
        scratch_shapes=[
            pltpu.VMEM((2, blk_cols * NUB, lanes), f32),
            pltpu.VMEM((2, side, side), f32),
            pltpu.VMEM((modes, side, 2 * side), f32),
            pltpu.VMEM((side, side), f32),
            pltpu.VMEM((2, side, side), f32),
        ],
        compiler_params=pltpu.CompilerParams(vmem_limit_bytes=VMEM_BYTES),
    )(
        window_corners.reshape(2),
        gathered.reshape(n_slab, NUB, rows, z_cells),
        illumination_modes,
        observed_power[0, 0],
        tables(side),
    )

    planes = 2 * modes // n_angle
    vin, probe_grad = pl.pallas_call(
        functools.partial(reduce_kernel, n_slab, n_angle),
        out_shape=(
            jax.ShapeDtypeStruct((n_angle, n_slab, rows, z_cells), f32),
            jax.ShapeDtypeStruct((2 * modes, per_slab, side), f32),
        ),
        in_specs=[VMEM, VMEM, SMEM],
        out_specs=(VMEM, VMEM),
        scratch_shapes=[
            pltpu.VMEM((n_out, MID, NUB, rows, z_cells), f32),
            pltpu.VMEM((n_out, MID, NUB, rows, z_cells), f32),
            pltpu.VMEM((n_out, NUB, rows, z_cells), f32),
            pltpu.VMEM((n_out, NUB, rows, z_cells), f32),
            pltpu.VMEM((n_out, NUB, rows, z_cells), f32),
            pltpu.VMEM((2 * modes, n_out, MID, per_slab, side), f32),
            pltpu.VMEM((2 * modes, n_out, MID, per_slab, side), f32),
            pltpu.VMEM((n_angle, planes, n_out, MID, per_slab, side), f32),
            pltpu.VMEM((planes, n_out, MID, per_slab, side), f32),
            pltpu.VMEM((planes, n_out, per_slab, side), f32),
            pltpu.VMEM((planes, n_out, per_slab, side), f32),
            pltpu.VMEM((n_out, planes, per_slab, side), f32),
            pltpu.VMEM((n_slab, n_angle, rows, z_cells), f32),
            pltpu.VMEM((n_angle, n_slab, rows, z_cells), f32),
            dma((2,)), dma((2,)),
            dma((n_out,)), dma((n_out,)),
            dma((n_slab,)), dma((n_slab,)),
            dma((n_angle,)), dma((n_angle,)),
            dma((2,)), dma((2,)),
            dma((n_angle,)), dma((n_angle,)),
            dma((n_out,)), dma((n_out,)),
            dma((n_angle,)), dma((n_angle,)),
        ],
        compiler_params=pltpu.CompilerParams(collective_id=1, has_side_effects=True, vmem_limit_bytes=VMEM_BYTES),
    )(
        grad.reshape(n_out, MID, INNER, NUB, rows, z_cells),
        pterm.reshape(2 * modes, n_out, MID, INNER, per_slab, side),
        hot,
    )
    incoming = vin.reshape(n_angle, 2, blk_cols, z_cells)
    tile_grad = jnp.einsum(
        "auk,acuz->ckz", resampling_matrices.astype(f32), incoming, precision=lax.Precision.HIGHEST
    )
    vol_grad = tile_grad.reshape(2, x_cells, y_here, z_cells)
    return (
        vol_grad,
        probe_grad.reshape(modes, 2, per_slab, side),
        resid[None, None],
        shift[None, None],
    )


def solution(mesh):
    in_specs = (
        P(None, "slab", "angle", None),
        P(),
        P(),
        P(),
        P("angle", "slab", None),
        P("angle", "slab", None, None),
    )
    out_specs = (
        P(None, "slab", "angle", None),
        P(None, None, "slab", None),
        P("angle", "slab", None, None),
        P("angle", "slab", None),
    )
    return jax.shard_map(local, mesh=mesh, in_specs=in_specs, out_specs=out_specs, check_vma=False)
```

profile of v0, /device:TPU:0, one launch (start us, length us, event | category | flops | bytes accessed | tf_op | source)
XLA Modules:
  0.0 97.3 jit_solution(8083577858922834054)
XLA Ops:
  0.6 0.0 copy-start
  0.6 0.0 copy-start.2
  0.7 0.0 copy-start.3
  0.7 0.0 copy-start.1
  0.7 0.9 copy-done
  1.6 0.7 constant_dynamic-slice_fusion
  2.2 0.1 copy.18
  2.3 0.1 eq.17
  2.4 0.1 fusion.2
  2.5 0.1 reshape.52.hot
  2.6 1.0 convolution_bitcast_fusion
  3.6 31.3 %shard_map.102 = f32[4,2,2,5,8,320]{5,4,3,2,1,0:T(8,128)S(1)} custom-call(f32[2,16,8,320]{3,2,1,0:T(8,128)S(1)} %bitcast.34, f32[160]{0:T(256)S(1)} %reshape.52.hot), custom_call_target="tpu_custom_call" | custom-call | tf_op jit(solution)/shard_map/pallas_call | solution.py:385
  34.9 0.0 copy-done.2
  34.9 0.0 copy-done.3
  34.9 0.0 copy-done.1
  34.9 19.8 %shard_map.103 = (f32[16,5,8,320]{3,2,1,0:T(8,128)S(1)}, f32[4,2,256,256]{3,2,1,0:T(8,128)S(1)}, f32[256,256]{1,0:T(8,128)}, f32[2]{0:T(128)}) custom-call(s32[2]{0:T(128)S(1)} %bitcast.39, f32[16,5,8,320]{3,2,1,0:T(8,128)S(1)} %bitcast.32, bf16[4,2,256,256]{3,2,1,0:T(8,128)(2,1)S(1)} %copy-done.1, f32[256,256]{1,0:T(8,128)S(1)} %bitcast.37, ...), custom_call_target="tpu_custom_call" | custom-call | tf_op jit(solution)/shard_map/pallas_call | solution.py:402
  54.7 0.0 copy-start.4
  54.7 40.5 %shard_map.104 = (f32[2,16,8,320]{3,2,1,0:T(8,128)S(1)}, f32[8,16,256]{2,1,0:T(8,128)S(1)}) custom-call(f32[4,2,2,5,8,320]{5,4,3,2,1,0:T(8,128)S(1)} %bitcast.35, f32[8,4,2,2,16,256]{5,4,3,2,1,0:T(8,128)S(1)} %bitcast.33, f32[160]{0:T(256)S(1)} %reshape.52.hot), custom_call_target="tpu_custom_call" | custom-call | tf_op jit(solution)/shard_map/pallas_call | solution.py:429
  95.2 0.0 copy-done.4
  95.2 0.5 convolution_bitcast_fusion.1
  95.7 0.9 copy.20
  96.6 0.7 copy.27
  (1 shorter events, 0.0 us)
Async XLA Ops:
  0.6 0.9 copy-start
  0.6 34.2 %copy-start.2 = (f32[1,1,256,256]{3,2,1,0:T(8,128)S(1)}, f32[1,1,256,256]{3,2,1,0:T(8,128)}, u32[]{:S(2)}) copy-start(f32[1,1,256,256]{3,2,1,0:T(8,128)} %param.12) | copy-start | bytes 786436
  0.7 34.2 %copy-start.3 = (s32[1,1,2]{2,1,0:T(1,128)S(1)}, s32[1,1,2]{2,1,0:T(1,128)}, u32[]{:S(2)}) copy-start(s32[1,1,2]{2,1,0:T(1,128)} %param.11) | copy-start | bytes 28
  0.7 34.2 %copy-start.1 = (bf16[4,2,256,256]{3,2,1,0:T(8,128)(2,1)S(1)}, bf16[4,2,256,256]{3,2,1,0:T(8,128)(2,1)}, u32[]{:S(2)}) copy-start(bf16[4,2,256,256]{3,2,1,0:T(8,128)(2,1)} %probe.1) | copy-start | bytes 3145732
  54.7 40.5 %copy-start.4 = (bf16[2,64,128]{2,1,0:T(8,128)(2,1)S(1)}, bf16[2,64,128]{2,1,0:T(8,128)(2,1)}, u32[]{:S(2)}) copy-start(bf16[2,64,128]{2,1,0:T(8,128)(2,1)} %param.8) | copy-start | bytes 98308
where the time goes:
time: 97.5 us; the launch traced here: 97.3 us
  Pallas kernels  91.6 us (94%)
  local copies, waits for them, and re-layouts  3.47 us (4%)
  matrix products  1.43 us (1%)
    pallas_call x1, Pallas kernels, local(): pl.pallas_call(functools.partial(reduce_kernel, n_slab, n_angle), out_sha...  40.5 us
    pallas_call x1, Pallas kernels, local(): pl.pallas_call(functools.partial(gather_kernel, n_slab, n_angle), out_sha...  31.3 us
    pallas_call x1, Pallas kernels, local(): pl.pallas_call(spot_kernel, out_shape=(jax.ShapeDtypeStruct((n_slab, NUB,...  19.8 us

commit v1 on v0

v1 whole, which is shorter than its diff:
```python
import functools
import math

import jax
import jax.numpy as jnp
import numpy as np
from jax import lax
from jax.experimental import pallas as pl
from jax.experimental.pallas import tpu as pltpu
from jax.sharding import PartitionSpec as P

NUB = 5
INNER = 2
MID = 2
MESH = pl.DeviceIdType.MESH
VMEM = pl.BlockSpec(memory_space=pltpu.VMEM)
SMEM = pl.BlockSpec(memory_space=pltpu.SMEM)
VMEM_BYTES = 48 * 1024 * 1024


def others(n_slab, n_angle, me_s, me_a, visit):
    for turn in range(1, n_angle + 1):
        step = turn % n_angle
        peer_a = lax.rem(me_a + step, n_angle)

        @pl.loop(1 if step == 0 else 0, n_slab)
        def _(off):
            visit(step, off, {"slab": lax.rem(me_s + off, n_slab), "angle": peer_a})


def greet(n_slab, n_angle, me_s, me_a):
    barrier = pltpu.get_barrier_semaphore()
    others(
        n_slab, n_angle, me_s, me_a,
        lambda step, off, device: pl.semaphore_signal(barrier, inc=1, device_id=device, device_id_type=MESH),
    )
    pl.semaphore_wait(barrier, n_slab * n_angle - 1)


def send(src, dst, send_sem, recv_sem, device):
    return pltpu.make_async_remote_copy(
        src_ref=src, dst_ref=dst, send_sem=send_sem, recv_sem=recv_sem, device_id=device, device_id_type=MESH
    )


def gather_kernel(n_slab, n_angle, blocks, hot, out, got, as_, ar, zs, zr, ys, yr, cs, cr):
    n_out = n_slab // (MID * INNER)
    me_s, me_a = lax.axis_index("slab"), lax.axis_index("angle")
    me_z, me_y, me_c = me_s // (MID * INNER), lax.rem(me_s // INNER, MID), lax.rem(me_s, INNER)
    greet(n_slab, n_angle, me_s, me_a)

    def acopy(step, off, device):
        src = blocks.at[device["angle"], device["slab"]]
        return send(src, got.at[me_a, me_s], as_.at[step, off], ar.at[step, off], device)

    others(n_slab, n_angle, me_s, me_a, lambda *at: acopy(*at).start())
    got[me_a, me_s] = blocks[me_a, me_s]
    others(n_slab, n_angle, me_s, me_a, lambda *at: acopy(*at).wait_recv())

    rows, z_cells = blocks.shape[2], blocks.shape[3]

    def add(i, acc):
        for j in range(n_angle):
            item = got[j, i]
            acc = tuple(acc[d] + hot[(i * n_angle + j) * NUB + d] * item for d in range(NUB))
        return acc

    acc = lax.fori_loop(0, n_slab, add, tuple(jnp.zeros((rows, z_cells), jnp.float32) for _ in range(NUB)))
    for d in range(NUB):
        out[me_z, me_y, me_c, d] = acc[d]

    def to_slab(z, y, c):
        return {"slab": (z * MID + y) * INNER + c}

    def zcopy(off):
        piece = out.at[me_z, me_y, me_c]
        return send(piece, piece, zs.at[off], zr.at[off], to_slab(lax.rem(me_z + off, n_out), me_y, me_c))

    def ycopy(off):
        piece = out.at[lax.rem(me_z + n_out - off, n_out), me_y, me_c]
        return send(piece, piece, ys.at[off], yr.at[off], to_slab(me_z, 1 - me_y, me_c))

    def ccopy(off, flip):
        row = 1 - me_y if flip else me_y
        piece = out.at[lax.rem(me_z + n_out - off, n_out), row, me_c]
        return send(piece, piece, cs.at[flip, off], cr.at[flip, off], to_slab(me_z, me_y, 1 - me_c))

    ycopy(0).start()
    for off in range(1, n_out):
        zcopy(off).start()
    ccopy(0, 0).start()
    for off in range(1, n_out):
        zcopy(off).wait_recv()
        ycopy(off).start()
        ccopy(off, 0).start()
    for off in range(n_out):
        ycopy(off).wait_recv()
        ccopy(off, 1).start()
    for off in range(n_out):
        ccopy(off, 0).wait_recv()
        ccopy(off, 1).wait_recv()
        ycopy(off).wait_send()
        ccopy(off, 0).wait_send()
        ccopy(off, 1).wait_send()
    for off in range(1, n_out):
        zcopy(off).wait_send()
    others(n_slab, n_angle, me_s, me_a, lambda *at: acopy(*at).wait_send())


def split(x):
    high = x.astype(jnp.bfloat16)
    return high, (x - high.astype(jnp.float32)).astype(jnp.bfloat16)


def dot3(a, b):
    def dot(x, y):
        return jnp.dot(x, y, preferred_element_type=jnp.float32)

    return dot(a[0], b[0]) + (dot(a[0], b[1]) + dot(a[1], b[0]))


def adjoint_kernel(
    n_slab, n_angle, far, resid, trans, det, probe, tabs, hot, corner, vin, pr, shift,
    tgrad, pg, p1, s1, p2, s2, p3, disp, q, q1, t1, q2x, t2x, q2y, t2y, q3y, q3x, t3, q4,
    pcs, pcr, pys, pyr, pzs, pzr, ds, dr, qcs, qcr, qxs, qxr, qys, qyr, qzs, qzr, qgs, qgr,
):
    n_out = n_slab // (MID * INNER)
    modes, _, side, _ = probe.shape
    rows, z_cells = disp.shape[2], disp.shape[3]
    per = q.shape[4]
    groups = q1.shape[0]
    me_s, me_a = lax.axis_index("slab"), lax.axis_index("angle")
    me_z, me_y, me_c = me_s // (MID * INNER), lax.rem(me_s // INNER, MID), lax.rem(me_s, INNER)
    greet(n_slab, n_angle, me_s, me_a)

    def to_slab(z, y, c):
        return {"slab": (z * MID + y) * INNER + c}

    core_peer = to_slab(me_z, me_y, 1 - me_c)
    mid_peer = to_slab(me_z, 1 - me_y, me_c)

    def at_z(off):
        return lax.rem(me_z + off, n_out)

    def at_a(off):
        return lax.rem(me_a + off, n_angle)

    def qc(g):
        src = q.at[pl.ds(g * n_angle, n_angle), :, :, 1 - me_c]
        return send(src, q1.at[g], qcs.at[g], qcr.at[g], core_peer)

    def qx(g, off):
        src, dst = (t1.at[g, at_a(off)], q2x.at[g, off]) if g % 2 == 0 else (t2y.at[g, at_a(off)], q3x.at[g, off])
        return send(src, dst, qxs.at[g, off], qxr.at[g, off], {"angle": at_a(off)})

    def qy(g):
        src, dst = (t2x.at[g, :, 1 - me_y], q3y.at[g]) if g % 2 == 0 else (t1.at[g, :, :, 1 - me_y], q2y.at[g])
        return send(src, dst, qys.at[g], qyr.at[g], mid_peer)

    def qz(g, off):
        return send(t3.at[g, at_z(off)], q4.at[g, off], qzs.at[g, off], qzr.at[g, off], to_slab(at_z(off), me_y, me_c))

    def qg(g, off):
        plane = pr.at[g * n_angle + me_a]
        return send(plane, plane, qgs.at[g, off], qgr.at[g, off], {"angle": at_a(off)})

    def start_x(g):
        for off in range(1, n_angle):
            qx(g, off).start()

    def sum_x(g, own, parts):
        total = own
        for off in range(1, n_angle):
            qx(g, off).wait_recv()
            total = total + parts[g, off]
        return total

    def after_core(g):
        qc(g).wait_recv()
        t1[g] = q[g * n_angle : (g + 1) * n_angle, :, :, me_c] + q1[g]
        if g % 2 == 0:
            start_x(g)
        else:
            qy(g).start()

    def after_first(g):
        if g % 2 == 0:
            t2x[g] = sum_x(g, t1[g, me_a], q2x)
            qy(g).start()
        else:
            qy(g).wait_recv()
            t2y[g] = t1[g, :, :, me_y] + q2y[g]
            start_x(g)

    def after_second(g):
        if g % 2 == 0:
            qy(g).wait_recv()
            t3[g] = t2x[g, :, me_y] + q3y[g]
        else:
            t3[g] = sum_x(g, t2y[g, me_a], q3x)
        for off in range(1, n_out):
            qz(g, off).start()

    def after_z(g):
        total = t3[g, me_z]
        for off in range(1, n_out):
            qz(g, off).wait_recv()
            total = total + q4[g, off]
        pr[g * n_angle + me_a] = total
        for off in range(1, n_angle):
            qg(g, off).start()

    left = (tabs[0], tabs[1])
    right = (tabs[2], tabs[3])
    tgrad[...] = jnp.zeros_like(tgrad)
    weight = 2.0 * resid[...]
    for m in range(modes):
        pull = jnp.concatenate([far[m, :, :side] * weight, far[m, :, side:] * weight], axis=0)
        mid = dot3(right, split(pull))
        both = jnp.concatenate([mid[:side], mid[side:]], axis=1)
        back = dot3(split(both), left)
        er, ei = back[:, :side], back[:, side:]
        tr, ti = trans[0], trans[1]
        terms = (er * tr + ei * ti, ei * tr - er * ti)
        for part in range(2):
            for k in range(n_slab):
                z, y, c = k // (MID * INNER), k // INNER % MID, k % INNER
                q[2 * m + part, z, y, c] = terms[part][k * per : (k + 1) * per]
        pr_, pi_ = probe[m, 0].astype(jnp.float32), probe[m, 1].astype(jnp.float32)
        tgrad[0] += pr_ * er + pi_ * ei
        tgrad[1] += pr_ * ei - pi_ * er
        if 2 * (m + 1) % n_angle == 0:
            g = 2 * (m + 1) // n_angle - 1
            qc(g).start()
            if g >= 1:
                after_core(g - 1)
            if g >= 3:
                after_first(g - 3)

    tr, ti = trans[0], trans[1]
    ga, gb = tgrad[0], tgrad[1]
    patch = (gb * tr - ga * ti, -(ga * tr + gb * ti))
    det_cols, lanes = det.shape[1], det.shape[2]
    to_col = (
        lax.broadcasted_iota(jnp.int32, (det_cols, side), 0)
        == lax.broadcasted_iota(jnp.int32, (det_cols, side), 1) + corner[0]
    ).astype(jnp.float32).astype(jnp.bfloat16)
    to_row = (
        lax.broadcasted_iota(jnp.int32, (side, lanes), 0) + corner[1]
        == lax.broadcasted_iota(jnp.int32, (side, lanes), 1)
    ).astype(jnp.float32).astype(jnp.bfloat16)
    per_comp = n_slab // 2
    for c in range(2):
        wide = jnp.dot(to_col, jnp.concatenate(split(patch[c]), axis=1), preferred_element_type=jnp.float32)
        wide = wide.astype(jnp.bfloat16)
        placed = jnp.dot(wide[:, :side], to_row, preferred_element_type=jnp.float32) + jnp.dot(
            wide[:, side:], to_row, preferred_element_type=jnp.float32
        )
        for k in range(c * per_comp, (c + 1) * per_comp):
            z, y, core = k // (MID * INNER), k // INNER % MID, k % INNER
            for d in range(NUB):
                at = (d * per_comp + k % per_comp) * rows
                pg[z, y, core, d] = placed[at : at + rows, :z_cells]

    def pc(off):
        return send(pg.at[at_z(off), :, 1 - me_c], p1.at[off], pcs.at[off], pcr.at[off], core_peer)

    def py(off):
        return send(s1.at[off, 1 - me_y], p2.at[off], pys.at[off], pyr.at[off], mid_peer)

    def pz(off):
        return send(s2.at[off], p3.at[off], pzs.at[off], pzr.at[off], to_slab(at_z(off), me_y, me_c))

    turns = tuple(range(1, n_out)) + (0,)
    for off in turns:
        pc(off).start()
    for off in turns:
        pc(off).wait_recv()
        s1[off] = pg[at_z(off), :, me_c] + p1[off]
        py(off).start()
    after_core(groups - 1)
    for g in range(max(groups - 3, 0), groups - 1):
        after_first(g)
    for c in range(2):
        here = det[c]
        dcol = pltpu.roll(here, det_cols - 1, 0)[:side, :side] - pltpu.roll(here, 1, 0)[:side, :side]
        drow = pltpu.roll(here, lanes - 1, 1)[:side, :side] - pltpu.roll(here, 1, 1)[:side, :side]
        moved = (jnp.sum(patch[c] * dcol) * 0.5 / side, jnp.sum(patch[c] * drow) * 0.5 / side)
        for axis in range(2):
            shift[axis] = moved[axis] if c == 0 else shift[axis] + moved[axis]
    for off in turns:
        py(off).wait_recv()
        s2[off] = s1[off, me_y] + p2[off]
        if off:
            pz(off).start()
    after_first(groups - 1)
    for g in range(groups - 1):
        after_second(g)
    total = s2[0]
    for off in range(1, n_out):
        pz(off).wait_recv()
        total = total + p3[off]

    @pl.loop(0, n_slab)
    def _(i):
        for j in range(n_angle):
            base = (i * n_angle + j) * NUB
            block = hot[base] * total[0]
            for d in range(1, NUB):
                block = block + hot[base + d] * total[d]
            disp[i, j] = block

    def dcopy(step, off, device):
        src = disp.at[device["slab"], device["angle"]]
        return send(src, vin.at[me_a, me_s], ds.at[step, off], dr.at[step, off], device)

    others(n_slab, n_angle, me_s, me_a, lambda *at: dcopy(*at).start())
    vin[me_a, me_s] = disp[me_s, me_a]
    after_second(groups - 1)
    for g in range(groups):
        after_z(g)
    others(n_slab, n_angle, me_s, me_a, lambda *at: dcopy(*at).wait_recv())
    for g in range(groups):
        for off in range(1, n_angle):
            qg(g, off).wait_recv()
            qg(g, off).wait_send()
            qx(g, off).wait_send()
        qc(g).wait_send()
        qy(g).wait_send()
        for off in range(1, n_out):
            qz(g, off).wait_send()
    for off in range(n_out):
        pc(off).wait_send()
        py(off).wait_send()
        if off:
            pz(off).wait_send()
    others(n_slab, n_angle, me_s, me_a, lambda *at: dcopy(*at).wait_send())


def spot_kernel(corner, gathered, probe, power, tabs, inten, far, trans, det):
    n_slab, _, rows, z_cells = gathered.shape
    side = probe.shape[2]
    modes = probe.shape[0]
    det_cols = det.shape[1]
    lanes = det.shape[2]
    per = n_slab // 2
    cols = per * rows
    col, row = corner[0], corner[1]
    for k in range(n_slab):
        for d in range(NUB):
            at = d * cols + (k % per) * rows
            det[k // per, at : at + rows, :z_cells] = gathered[k, d]
    for c in range(2):
        det[c, :, z_cells:] = jnp.zeros((det_cols, lanes - z_cells), jnp.float32)
        moved = pltpu.roll(det[c], lanes - row, 1)
        det[c] = pltpu.roll(moved, det_cols - col, 0)
    absorb = jnp.exp(-det[1, :side, :side])
    phase = det[0, :side, :side]
    trans[0] = absorb * jnp.cos(phase)
    trans[1] = absorb * jnp.sin(phase)
    inten[...] = -power[...]
    left = (tabs[0], tabs[1])
    right = (tabs[2], tabs[3])

    @pl.loop(0, modes)
    def _(m):
        pr_, pi_ = probe[m, 0].astype(jnp.float32), probe[m, 1].astype(jnp.float32)
        tr, ti = trans[0], trans[1]
        stacked = jnp.concatenate([pr_ * tr - pi_ * ti, pr_ * ti + pi_ * tr], axis=0)
        mid = dot3(left, split(stacked))
        both = jnp.concatenate([mid[:side], mid[side:]], axis=1)
        field = dot3(split(both), right)
        far[m] = field
        fr, fi = field[:, :side], field[:, side:]
        inten[...] += fr * fr + fi * fi


def tables(length):
    ids = np.outer(np.arange(length), np.arange(length)) % length
    phases = ids * (2.0 * math.pi / length)
    c, s = np.cos(phases) / math.sqrt(length), np.sin(phases) / math.sqrt(length)
    left = np.block([[c, s], [-s, c]])
    parts = []
    for table in (left, left.T):
        high = table.astype(jnp.bfloat16)
        parts += [high, (table - high.astype(np.float64)).astype(jnp.bfloat16)]
    return jnp.asarray(np.stack(parts))


def local(object_density, resampling_matrices, receiving_tile_number, illumination_modes, window_corners, observed_power):
    n_angle = lax.axis_size("angle")
    n_slab = lax.axis_size("slab")
    n_out = n_slab // (MID * INNER)
    my_angle = lax.axis_index("angle")
    x_cells = object_density.shape[1]
    y_here = object_density.shape[2]
    z_cells = object_density.shape[3]
    tile_rows = resampling_matrices.shape[2]
    blk_cols = resampling_matrices.shape[1]
    modes, _, side, _ = illumination_modes.shape
    rows = 2 * blk_cols // n_slab
    per_slab = side // n_slab
    lanes = (z_cells + 127) // 128 * 128
    f32 = jnp.float32
    dma = pltpu.SemaphoreType.DMA

    tile = object_density.reshape(2, tile_rows, z_cells)
    blocks = jnp.einsum("auk,ckz->acuz", resampling_matrices, tile, preferred_element_type=f32)
    blocks = blocks.reshape(n_angle, n_slab, rows, z_cells)
    ids = lax.dynamic_index_in_dim(receiving_tile_number, my_angle, 0, keepdims=False).reshape(-1)
    hot = (ids[:, None] == jnp.arange(NUB, dtype=jnp.int32)[None, :]).astype(f32).reshape(-1)

    gathered = pl.pallas_call(
        functools.partial(gather_kernel, n_slab, n_angle),
        out_shape=jax.ShapeDtypeStruct((n_out, MID, INNER, NUB, rows, z_cells), f32),
        in_specs=[VMEM, SMEM],
        out_specs=VMEM,
        scratch_shapes=[
            pltpu.VMEM((n_angle, n_slab, rows, z_cells), f32),
            dma((n_angle, n_slab)), dma((n_angle, n_slab)),
            dma((n_out,)), dma((n_out,)),
            dma((n_out,)), dma((n_out,)),
            dma((2, n_out)), dma((2, n_out)),
        ],
        compiler_params=pltpu.CompilerParams(collective_id=0, has_side_effects=True, vmem_limit_bytes=VMEM_BYTES),
    )(blocks, hot)

    tabs = tables(side)
    corner = window_corners.reshape(2)
    resid, far, trans, det = pl.pallas_call(
        spot_kernel,
        out_shape=(
            jax.ShapeDtypeStruct((side, side), f32),
            jax.ShapeDtypeStruct((modes, side, 2 * side), f32),
            jax.ShapeDtypeStruct((2, side, side), f32),
            jax.ShapeDtypeStruct((2, blk_cols * NUB, lanes), f32),
        ),
        in_specs=[SMEM, VMEM, VMEM, VMEM, VMEM],
        out_specs=(VMEM, VMEM, VMEM, VMEM),
        compiler_params=pltpu.CompilerParams(vmem_limit_bytes=VMEM_BYTES),
    )(corner, gathered.reshape(n_slab, NUB, rows, z_cells), illumination_modes, observed_power[0, 0], tabs)

    groups = 2 * modes // n_angle
    shapes = (
        (2, side, side),
        (n_out, MID, INNER, NUB, rows, z_cells),
        (n_out, MID, NUB, rows, z_cells),
        (n_out, MID, NUB, rows, z_cells),
        (n_out, NUB, rows, z_cells),
        (n_out, NUB, rows, z_cells),
        (n_out, NUB, rows, z_cells),
        (n_slab, n_angle, rows, z_cells),
        (2 * modes, n_out, MID, INNER, per_slab, side),
        (groups, n_angle, n_out, MID, per_slab, side),
        (groups, n_angle, n_out, MID, per_slab, side),
        (groups, n_angle, n_out, MID, per_slab, side),
        (groups, n_out, MID, per_slab, side),
        (groups, n_angle, n_out, per_slab, side),
        (groups, n_angle, n_out, per_slab, side),
        (groups, n_out, per_slab, side),
        (groups, n_angle, n_out, per_slab, side),
        (groups, n_out, per_slab, side),
        (groups, n_out, per_slab, side),
    )
    sems = (
        (n_out,), (n_out,), (n_out,), (n_angle, n_slab),
        (groups,), (groups, n_angle), (groups,), (groups, n_out), (groups, n_angle),
    )
    vin, probe_grad, shift = pl.pallas_call(
        functools.partial(adjoint_kernel, n_slab, n_angle),
        out_shape=(
            jax.ShapeDtypeStruct((n_angle, n_slab, rows, z_cells), f32),
            jax.ShapeDtypeStruct((2 * modes, per_slab, side), f32),
            jax.ShapeDtypeStruct((2,), f32),
        ),
        in_specs=[VMEM] * 6 + [SMEM, SMEM],
        out_specs=(VMEM, VMEM, SMEM),
        scratch_shapes=[pltpu.VMEM(shape, f32) for shape in shapes] + [dma(shape) for shape in sems for _ in range(2)],
        compiler_params=pltpu.CompilerParams(collective_id=1, has_side_effects=True, vmem_limit_bytes=VMEM_BYTES),
    )(far, resid, trans, det, illumination_modes, tabs, hot, corner)
    incoming = vin.reshape(n_angle, 2, blk_cols, z_cells)
    tile_grad = jnp.einsum(
        "auk,acuz->ckz", resampling_matrices.astype(f32), incoming, precision=lax.Precision.HIGHEST
    )
    vol_grad = tile_grad.reshape(2, x_cells, y_here, z_cells)
    return (
        vol_grad,
        probe_grad.reshape(modes, 2, per_slab, side),
        resid[None, None],
        shift[None, None],
    )


def solution(mesh):
    in_specs = (
        P(None, "slab", "angle", None),
        P(),
        P(),
        P(),
        P("angle", "slab", None),
        P("angle", "slab", None, None),
    )
    out_specs = (
        P(None, "slab", "angle", None),
        P(None, None, "slab", None),
        P("angle", "slab", None, None),
        P("angle", "slab", None),
    )
    return jax.shard_map(local, mesh=mesh, in_specs=in_specs, out_specs=out_specs, check_vma=False)
```

time: 97.5 us -> 96.2 us (0.987)
  Pallas kernels: 91.6 us -> 88.7 us
  local copies, waits for them, and re-layouts: 3.47 us -> 4.93 us
    pallas_call x2, Pallas kernels: 60.3 us -> 58.5 us  [the longest x1 47 us: local(): pl.pallas_call(functools.partial(adjoint_kernel, n_slab, n_angle), out_sh...]
    unnamed x11 -> x14, local copies, waits for them, and re-layouts: 1.57 us -> 3.02 us
    pallas_call x1, Pallas kernels: 31.3 us -> 30.2 us  [local(): pl.pallas_call(functools.partial(gather_kernel, n_slab, n_angle), out_sha...]
where the time goes in v1:
time: 96.2 us; the launch traced here: 95.9 us
  Pallas kernels  88.7 us (92%)
  local copies, waits for them, and re-layouts  4.93 us (5%)
  matrix products  1.43 us (1%)
    pallas_call x1, Pallas kernels, local(): pl.pallas_call(functools.partial(adjoint_kernel, n_slab, n_angle), out_sh...  47 us
    pallas_call x1, Pallas kernels, local(): pl.pallas_call(functools.partial(gather_kernel, n_slab, n_angle), out_sha...  30.2 us
    pallas_call x1, Pallas kernels, local(): pl.pallas_call(spot_kernel, out_shape=(jax.ShapeDtypeStruct((side, side),...  11.5 us
    unnamed x14, local copies, waits for them, and re-layouts  3.02 us

profile of v1, /device:TPU:0, one launch (start us, length us, event | category | flops | bytes accessed | tf_op | source)
XLA Modules:
  0.0 95.9 jit_solution(1327964159242585819)
XLA Ops:
  0.6 0.0 copy-start
  0.6 0.0 copy-start.1
  0.7 0.0 copy-start.2
  0.7 0.0 copy-start.4
  0.7 0.9 copy-done
  1.6 0.7 constant_dynamic-slice_fusion
  2.2 0.1 copy.18
  2.3 0.1 eq.17
  2.4 0.1 fusion.2
  2.5 0.1 reshape.44.hot
  2.6 1.0 convolution_bitcast_fusion
  3.6 30.2 %shard_map.102 = f32[4,2,2,5,8,320]{5,4,3,2,1,0:T(8,128)S(1)} custom-call(f32[2,16,8,320]{3,2,1,0:T(8,128)S(1)} %bitcast.31, f32[160]{0:T(256)S(1)} %reshape.44.hot), custom_call_target="tpu_custom_call" | custom-call | tf_op jit(solution)/shard_map/pallas_call | solution.py:413
  33.8 0.0 copy-done.1
  33.8 0.0 copy-done.2
  33.8 0.0 copy-done.4
  33.8 11.5 %shard_map.103 = (f32[256,256]{1,0:T(8,128)}, f32[4,256,512]{2,1,0:T(8,128)S(1)}, f32[2,256,256]{2,1,0:T(8,128)S(1)}, f32[2,320,384]{2,1,0:T(8,128)S(1)}) custom-call(s32[2]{0:T(128)S(1)} %bitcast.36, f32[16,5,8,320]{3,2,1,0:T(8,128)S(1)} %bitcast.30, bf16[4,2,256,256]{3,2,1,0:T(8,128)(2,1)S(1)} %copy-done.1, f32[256,256]{1,0:T(8,128)S(1)} %bitcast.33, ...), custom_call_target="tpu_custom_call" | custom-call | tf_op jit(solution)/shard_map/pallas_call | solution.py:430
  45.3 0.0 copy-start.3
  45.3 0.9 copy-done.3
  46.3 0.0 copy-start.5
  46.3 47.0 %shard_map.104 = (f32[2,16,8,320]{3,2,1,0:T(8,128)S(1)}, f32[8,16,256]{2,1,0:T(8,128)S(1)}, f32[2]{0:T(128)S(1)}) custom-call(f32[4,256,512]{2,1,0:T(8,128)S(1)} %get-tuple-element.11.far, f32[256,256]{1,0:T(8,128)S(1)} %copy-done.3, f32[2,256,256]{2,1,0:T(8,128)S(1)} %get-tuple-element.13.trans, f32[2,320,384]{2,1,0:T(8,128)S(1)} %get-tuple-element.14.det, ...), custom_call_target="tpu_custom_call" | custom-call | tf_op jit(solution)/shard_map/pallas_call | solution.py:469
  93.3 0.0 copy-done.5
  93.3 0.5 convolution_bitcast_fusion.1
  93.8 0.9 copy.20
  94.7 0.7 copy.28
  95.4 0.5 copy.29
  (1 shorter events, 0.0 us)
Async XLA Ops:
  0.6 0.9 copy-start
  0.6 33.2 %copy-start.1 = (bf16[4,2,256,256]{3,2,1,0:T(8,128)(2,1)S(1)}, bf16[4,2,256,256]{3,2,1,0:T(8,128)(2,1)}, u32[]{:S(2)}) copy-start(bf16[4,2,256,256]{3,2,1,0:T(8,128)(2,1)} %probe.3) | copy-start | bytes 3145732
  0.7 33.2 %copy-start.2 = (f32[1,1,256,256]{3,2,1,0:T(8,128)S(1)}, f32[1,1,256,256]{3,2,1,0:T(8,128)}, u32[]{:S(2)}) copy-start(f32[1,1,256,256]{3,2,1,0:T(8,128)} %param.12) | copy-start | bytes 786436
  0.7 33.2 %copy-start.4 = (s32[1,1,2]{2,1,0:T(1,128)S(1)}, s32[1,1,2]{2,1,0:T(1,128)}, u32[]{:S(2)}) copy-start(s32[1,1,2]{2,1,0:T(1,128)} %param.11) | copy-start | bytes 28
  45.3 0.9 copy-start.3
  46.3 47.0 %copy-start.5 = (bf16[2,64,128]{2,1,0:T(8,128)(2,1)S(1)}, bf16[2,64,128]{2,1,0:T(8,128)(2,1)}, u32[]{:S(2)}) copy-start(bf16[2,64,128]{2,1,0:T(8,128)(2,1)} %param.8) | copy-start | bytes 98308
